TPU v7x, 128 devices: a whole 4x4x4 slice. The times are simulated.
128 devices in a mesh: band: 64 (over y_lo, z, x, core), feat: 2 (over y_hi).
Axes of the slice: x: 4, y: 4 (y_hi: 2, y_lo: 2; y = y_hi * 2 + y_lo), z: 4, core: 2. Of those that a mesh axis runs over, the one named last changes fastest.
Arguments:
- grid_feat: bfloat16 [131072, 1024], P('band'), may hold values from -6 to 6
- mesh_feat: bfloat16 [32768, 1024], P('band'), may hold values from -6 to 6
- edge_src: int32 [524288], P('band'), may hold values from 0 to 2047
- edge_dst: int32 [524288], P('band'), may hold values from 0 to 1535, as said below
- w_grid: bfloat16 [1024, 1024], P(None, 'feat'), may hold values from -0.1875 to 0.1875
- w_mesh: bfloat16 [1024, 1024], P(None, 'feat'), may hold values from -0.1875 to 0.1875
- b_edge: bfloat16 [1024], P('feat'), may hold values from -4 to 4
- w_enc_out: bfloat16 [1024, 1024], P('feat'), may hold values from -0.046875 to 0.046875
- b_enc: bfloat16 [1024], replicated, may hold values from -3 to 3
- ln_gain: bfloat16 [1024], replicated, may hold values from 0.25 to 1.75
- w_query: bfloat16 [1024, 1024], P(None, 'feat')
- w_key: bfloat16 [1024, 1024], P(None, 'feat')
- w_value: bfloat16 [1024, 1024], P(None, 'feat'), may hold values from -0.1875 to 0.1875
- w_out: bfloat16 [1024, 1024], P('feat'), may hold values from -0.75 to 0.75
- b_out: bfloat16 [1024], replicated, may hold values from -3 to 3
Outputs:
- mesh_out: bfloat16 [32768, 1024], P('band', 'feat')
Inputs may be any that keep to these rules, and one draw needn't show every extreme that they name: Every edge's target lies in a band that exists: edges of band 0 have edge_dst of 512 or more, edges of the last band less than 1024.
All inputs are finite; a program needn't handle non-finite values.
Results may differ from a plain program's by a relative error of at most 0.0096.
The roundings to bfloat16 on the way count: a program that leaves them out, or rounds other values in their place, can miss the bound.
Values may be sent and summed in bfloat16 or wider, within the bound.
A program may use at most 128 MiB of HBM per device.

v0:
```python
import jax
import jax.numpy as jnp
from jax import lax
from jax.sharding import PartitionSpec as P

HEAD = 64


def with_halo(block, sides, width):
    for axis, dim in sides:
        count = lax.axis_size(axis)
        forward = [(i, i + 1) for i in range(count - 1)]
        backward = [(target, source) for source, target in forward]
        low = lax.ppermute(
            lax.slice_in_dim(block, block.shape[dim] - width, None, axis=dim), axis, forward
        )
        high = lax.ppermute(lax.slice_in_dim(block, 0, width, axis=dim), axis, backward)
        block = jnp.concatenate([low, block, high], axis=dim)
    return block


def passed_along(value, axis, steps):
    count = lax.axis_size(axis)
    initial, last = (max(0, -steps), min(count, count - steps))
    return lax.ppermute(value, axis, [(source, source + steps) for source in range(initial, last)])


def own_columns(array, start, count):
    return lax.dynamic_slice_in_dim(array, start, count, array.ndim - 1)


def body(
    grid_feat,
    mesh_feat,
    edge_src,
    edge_dst,
    w_grid,
    w_mesh,
    b_edge,
    w_enc_out,
    b_enc,
    ln_gain,
    w_query,
    w_key,
    w_value,
    w_out,
    b_out,
):
    mesh_rows = mesh_feat.shape[0]
    half_width = w_grid.shape[1]
    band_id = lax.axis_index("band")
    band_count = lax.axis_size("band")
    col_start = lax.axis_index("feat") * half_width
    grid_proj = jnp.dot(grid_feat, w_grid, preferred_element_type=jnp.float32)
    mesh_proj = jnp.dot(mesh_feat, w_mesh, preferred_element_type=jnp.float32).astype(jnp.bfloat16)
    window = with_halo(mesh_proj, (("band", 0),), mesh_rows)
    edge_input = (
        grid_proj[edge_src] + window[edge_dst].astype(jnp.float32) + b_edge.astype(jnp.float32)
    )
    hidden = jax.nn.silu(edge_input).astype(jnp.bfloat16)
    targets = jnp.arange(3 * mesh_rows, dtype=jnp.int32)
    onehot = (targets[:, None] == edge_dst[None, :]).astype(jnp.bfloat16)
    partial_value = jnp.dot(onehot, hidden, preferred_element_type=jnp.float32)
    from_above = passed_along(partial_value[2 * mesh_rows :], "band", 1)
    from_below = passed_along(partial_value[:mesh_rows], "band", -1)
    aggregate = partial_value[mesh_rows : 2 * mesh_rows] + from_above + from_below
    message = jnp.dot(aggregate.astype(jnp.bfloat16), w_enc_out, preferred_element_type=jnp.float32)
    summed = lax.psum(message, "feat")
    latent = mesh_feat.astype(jnp.float32) + summed + b_enc.astype(jnp.float32)
    row_mean = jnp.mean(latent, axis=1, keepdims=True)
    row_var = jnp.mean((latent - row_mean) ** 2, axis=1, keepdims=True)
    normed = (
        (latent - row_mean) * lax.rsqrt(row_var + 1e-05) * ln_gain.astype(jnp.float32)
    ).astype(jnp.bfloat16)
    latent_half = own_columns(latent, col_start, half_width)
    query = (jnp.dot(normed, w_query, preferred_element_type=jnp.float32) * HEAD ** (-0.5)).astype(
        jnp.bfloat16
    )
    key_rows = jnp.dot(normed, w_key, preferred_element_type=jnp.float32).astype(jnp.bfloat16)
    value_rows = jnp.dot(normed, w_value, preferred_element_type=jnp.float32).astype(jnp.bfloat16)
    paired = jnp.concatenate([key_rows, value_rows], axis=1)
    key_window = with_halo(paired, (("band", 0),), mesh_rows)
    heads_here = half_width // HEAD
    query_heads = query.reshape(mesh_rows, heads_here, HEAD)
    key_heads = key_window[:, :half_width].reshape(3 * mesh_rows, heads_here, HEAD)
    value_heads = key_window[:, half_width:].reshape(3 * mesh_rows, heads_here, HEAD)
    scores = jnp.einsum("qhd,khd->hqk", query_heads, key_heads, preferred_element_type=jnp.float32)
    neighbour = band_id + targets // mesh_rows - 1
    usable = (neighbour >= 0) & (neighbour < band_count)
    scores = jnp.where(usable[None, None, :], scores, jnp.float32(-1e30))
    row_max = jnp.max(scores, axis=2, keepdims=True)
    weights = jnp.exp(scores - row_max)
    row_total = jnp.sum(weights, axis=2, keepdims=True)
    attention = (weights / row_total).astype(jnp.bfloat16)
    mixed_heads = jnp.einsum(
        "hqk,khd->qhd", attention, value_heads, preferred_element_type=jnp.float32
    )
    mixed_heads = mixed_heads.reshape(mesh_rows, half_width).astype(jnp.bfloat16)
    projected = jnp.dot(mixed_heads, w_out, preferred_element_type=jnp.float32)
    out_part = lax.psum_scatter(projected, "feat", scatter_dimension=1, tiled=True)
    result = latent_half + out_part + own_columns(b_out, col_start, half_width).astype(jnp.float32)
    return result.astype(jnp.bfloat16)


def solution(mesh):
    placed = (
        P("band", None),
        P("band", None),
        P("band"),
        P("band"),
        P(None, "feat"),
        P(None, "feat"),
        P("feat"),
        P("feat", None),
        P(),
        P(),
        P(None, "feat"),
        P(None, "feat"),
        P(None, "feat"),
        P("feat", None),
        P(),
    )
    return jax.shard_map(
        body, mesh=mesh, in_specs=placed, out_specs=P("band", "feat"), check_vma=False
    )
```

profile of v0, /device:TPU:40, one launch (start us, length us, event | category | flops | bytes accessed | tf_op | source)
XLA Modules:
  0.0 319.7 jit_solution(17006869044423975580)
XLA Ops:
  6.5 2.3 convolution_convert_fusion.2
  8.9 0.0 copy-start.9
  8.9 0.0 copy-start.5
  8.9 3.7 %collective-permute-start.1 = (bf16[512,512]{1,0:T(8,128)(2,1)S(1)}, bf16[512,512]{1,0:T(8,128)(2,1)S(1)}, u32[]{:S(2)}, u32[]{:S(2)}) collective-permute-start(bf16[512,512]{1,0:T(8,128)(2,1)S(1)} %convolution_convert_fusion.2), channel_id=1, source_target_pairs={{2,0},{4,2},{6,4},{8,6},{10,8},{12,10},{14,12},{16,14},{18,16},{20... | collective-permute-start | bytes 1572872 | tf_op jit(solution)/shard_map/ppermute | solution.py:17
  12.6 1.9 collective-permute-start
  14.5 6.5 %fusion.38 = f32[2048,512]{1,0:T(8,128)} fusion(bf16[2048,1024]{1,0:T(8,128)(2,1)} %param.15, bf16[1024,512]{1,0:T(8,128)(2,1)S(1)} %copy-done), kind=kOutput, calls=%fused_computation.59 | convolution fusion | flops 2147483648 | bytes 9437184 | tf_op jit(solution)/shard_map/dot_general | solution.py:54
  21.0 0.0 copy-start.6
  21.0 37.2 %gather_fusion = f32[8192,512]{1,0:T(8,128)} fusion(f32[2048,512]{1,0:T(8,128)} %fusion.38, s32[8192]{0:T(1024)S(1)} %fusion.19), kind=kCustom, calls=%fused_computation | custom fusion | bytes 33587200 | tf_op jit(solution)/shard_map/gather | solution.py:58
  58.2 0.0 copy-start.4
  58.2 0.8 copy-done.4
  59.0 1.3 pad_maximum_fusion.1
  60.3 33.8 %gather_fusion.1 = bf16[8192,512]{1,0:T(8,128)(2,1)} fusion(bf16[1536,512]{1,0:T(8,128)(2,1)S(1)} %pad_maximum_fusion.1, s32[8192]{0:T(1024)S(1)} %fusion.20), kind=kCustom, calls=%fused_computation.1 | custom fusion | bytes 16809984 | tf_op jit(solution)/shard_map/gather | solution.py:58
  94.1 18.0 %fusion.1 = f32[1536,512]{1,0:T(8,128)S(1)} fusion(s32[8192]{0:T(1024)S(1)} %copy-done.6, f32[8192,512]{1,0:T(8,128)} %gather_fusion, bf16[8192,512]{1,0:T(8,128)(2,1)} %gather_fusion.1, f32[512]{0:T(512)S(1)} %convert_element_type.58), kind=kOutput, calls=%fused_computation.4 | convolution fusion | flops 12931039232 | bytes 28346368 | tf_op jit(solution)/shard_map/dot_general | solution.py:63
  112.1 0.0 copy-start.3
  112.1 0.2 fusion.36
  112.3 5.9 %collective-permute-start.3 = (f32[512,512]{1,0:T(8,128)S(1)}, f32[512,512]{1,0:T(8,128)S(1)}, u32[]{:S(2)}, u32[]{:S(2)}) collective-permute-start(f32[512,512]{1,0:T(8,128)S(1)} %get-tuple-element.10), channel_id=1, source_target_pairs={{2,0},{4,2},{6,4},{8,6},{10,8},{12,10},{14,12},{16,14},{18,16},{20... | collective-permute-start | bytes 3145736 | tf_op jit(solution)/shard_map/ppermute | solution.py:25
  118.2 0.0 copy-start.7
  118.2 0.0 copy-start.8
  118.2 1.9 collective-permute-start.2
  120.1 10.3 %collective-permute-done.3 = f32[512,512]{1,0:T(8,128)S(1)} collective-permute-done((f32[512,512]{1,0:T(8,128)S(1)}, f32[512,512]{1,0:T(8,128)S(1)}, u32[]{:S(2)}, u32[]{:S(2)}) %collective-permute-start.3) | collective-permute-done | bytes 1048608 | tf_op jit(solution)/shard_map/ppermute | solution.py:25
  130.5 6.0 %collective-permute-done.2 = f32[512,512]{1,0:T(8,128)S(1)} collective-permute-done((f32[512,512]{1,0:T(8,128)S(1)}, f32[512,512]{1,0:T(8,128)S(1)}, u32[]{:S(2)}, u32[]{:S(2)}) %collective-permute-start.2) | collective-permute-done | bytes 1048608 | tf_op jit(solution)/shard_map/ppermute | solution.py:25
  136.4 2.1 fusion.17
  138.5 0.0 all-reduce.2.cloned.1.call-update
  138.5 0.0 reduce-scatter.2.cloned.1.call-start
  138.6 74.3 %all-reduce.2.cloned.1.call-done = f32[512,1024]{1,0:T(8,128)} async-done(((f32[512,1024]{1,0:T(8,128)}), f32[512,1024]{1,0:T(8,128)}) %all-reduce.2.cloned.1.call-update) | async-done | bytes 2097168 | tf_op jit(solution)/shard_map/psum | solution.py:68
  212.9 2.2 fusion.34
  215.1 0.0 copy-start.11
  215.2 0.3 multiply_reduce_fusion
  215.5 0.3 multiply_convert_fusion.2
  215.9 0.5 copy-done.11
  216.4 0.8 convolution_convert_fusion
  217.1 0.8 convolution_convert_fusion.1
  217.9 1.0 pad_maximum_fusion.2
  218.9 3.9 %collective-permute-start.5 = (bf16[512,1024]{0,1:T(8,128)(2,1)}, bf16[512,1024]{0,1:T(8,128)(2,1)}, u32[]{:S(2)}, u32[]{:S(2)}) collective-permute-start(bf16[512,1024]{0,1:T(8,128)(2,1)} %pad_maximum_fusion.2), channel_id=1, source_target_pairs={{2,0},{4,2},{6,4},{8,6},{10,8},{12,10},{14,12},{16,14},{18,16},{20... | collective-permute-start | bytes 3145736 | tf_op jit(solution)/shard_map/ppermute | solution.py:17
  222.9 2.1 collective-permute-start.4
  225.0 3.1 fusion.10
  228.1 7.4 %collective-permute-done.5 = bf16[512,1024]{0,1:T(8,128)(2,1)} collective-permute-done((bf16[512,1024]{0,1:T(8,128)(2,1)}, bf16[512,1024]{0,1:T(8,128)(2,1)}, u32[]{:S(2)}, u32[]{:S(2)}) %collective-permute-start.5) | collective-permute-done | bytes 1048608 | tf_op jit(solution)/shard_map/ppermute | solution.py:17
  235.5 5.9 %collective-permute-done.4 = bf16[512,1024]{0,1:T(8,128)(2,1)} collective-permute-done((bf16[512,1024]{0,1:T(8,128)(2,1)}, bf16[512,1024]{0,1:T(8,128)(2,1)}, u32[]{:S(2)}, u32[]{:S(2)}) %collective-permute-start.4) | collective-permute-done | bytes 1048608 | tf_op jit(solution)/shard_map/ppermute | solution.py:14
  241.4 8.3 %pad_maximum_fusion = bf16[1536,1024]{0,1:T(8,128)(2,1)S(1)} fusion(bf16[512,1024]{0,1:T(8,128)(2,1)} %collective-permute-done.5, bf16[512,512]{0,1:T(8,128)(2,1)S(1)} %convolution_convert_fusion, bf16[512,512]{0,1:T(8,128)(2,1)S(1)} %convolution_convert_fusion.1, bf16[512,1024]{0,1:T(8,128)(2,1)} %collective-permute-done.4), kind=kLoop, calls=%fused_computation.14 | loop fusion | flops 12582912 | bytes 6291456 | tf_op jit(solution)/shard_map/concatenate | solution.py:18
  249.7 0.0 copy-start.13
  249.7 1.8 fusion.35
  251.6 8.3 %fusion.37 = f32[8,512]{1,0:T(8,128)S(1)} fusion(pred[1536]{0:T(1024)(128)(4,1)S(1)} %fusion.27, bf16[512,8,64]{0,2,1:T(8,128)(2,1)S(1)} %bitcast.28, bf16[1536,8,64]{0,2,1:T(8,128)(2,1)} %bitcast.24), kind=kOutput, calls=%fused_computation.58 | convolution fusion | flops 824182272 | bytes 2115072 | tf_op jit(solution)/shard_map/sub | solution.py:92
  259.9 11.8 %fusion.9 = bf16[8,64,512]{2,1,0:T(8,128)(2,1)} fusion(bf16[1536,8,64]{0,2,1:T(8,128)(2,1)} %bitcast.26, f32[8,512]{1,0:T(8,128)S(1)} %fusion.37, pred[1536]{0:T(1024)(128)(4,1)S(1)} %fusion.27, bf16[512,8,64]{0,2,1:T(8,128)(2,1)S(1)} %bitcast.29, bf16[1536,8,64]{0,2,1:T(8,128)(2,1)} %bitcast.25), kind=kOutput, calls=%fused_computation.21 | convolution fusion | flops 1636046336 | bytes 4212224 | tf_op jit(solution)/shard_map/hqk,khd->qhd/dot_general | solution.py:95
  271.7 3.5 %fusion.39 = f32[512,1024]{1,0:T(8,128)} fusion(bf16[512,512]{0,1:T(8,128)(2,1)} %bitcast.27, bf16[512,1024]{1,0:T(8,128)(2,1)} %param.28), kind=kOutput, calls=%fused_computation.60 | convolution fusion | flops 536870912 | bytes 3670016 | tf_op jit(solution)/shard_map/dot_general | solution.py:99
  275.2 0.0 reduce-scatter.2.cloned.1.call-update
  275.3 0.1 dynamic-slice_convert_fusion
  275.4 35.2 %reduce-scatter.2.cloned.1.call-done = f32[512,512]{1,0:T(8,128)} async-done(((f32[512,1024]{1,0:T(8,128)}), f32[512,512]{1,0:T(8,128)}) %reduce-scatter.2.cloned.1.call-update) | async-done | bytes 1048592 | tf_op jit(solution)/shard_map/reduce_scatter | solution.py:100
  310.6 2.3 add_convert_fusion
  (28 shorter events, 0.1 us)
Async XLA Ops:
  6.5 8.0 %copy-start = (bf16[1024,512]{1,0:T(8,128)(2,1)S(1)}, bf16[1024,512]{1,0:T(8,128)(2,1)}, u32[]{:S(2)}) copy-start(bf16[1024,512]{1,0:T(8,128)(2,1)} %param.19) | copy-start | bytes 3145732
  6.5 206.4 %all-reduce.2.cloned.1.call-start = ((), (), s32[]{:S(2)}) async-start(), calls=%async_computation.1 | async-start | bytes 4194304 | tf_op jit(solution)/shard_map/psum | solution.py:68
  8.9 12.1 %copy-start.9 = (bf16[512]{0:T(512)(128)(2,1)S(1)}, bf16[512]{0:T(512)(128)(2,1)}, u32[]{:S(2)}) copy-start(bf16[512]{0:T(512)(128)(2,1)} %param.21) | copy-start | bytes 3076
  8.9 12.1 %copy-start.5 = (s32[8192]{0:T(1024)S(1)}, s32[8192]{0:T(1024)}, u32[]{:S(2)}) copy-start(s32[8192]{0:T(1024)} %param.17) | copy-start | bytes 98308
  8.9 49.3 %collective-permute-start.1 = (bf16[512,512]{1,0:T(8,128)(2,1)S(1)}, bf16[512,512]{1,0:T(8,128)(2,1)S(1)}, u32[]{:S(2)}, u32[]{:S(2)}) collective-permute-start(bf16[512,512]{1,0:T(8,128)(2,1)S(1)} %convolution_convert_fusion.2), channel_id=1, source_target_pairs={{2,0},{4,2},{6,4},{8,6},{10,8},{12,10},{14,12},{16,14},{18,16},{20... | collective-permute-start | bytes 1572872 | tf_op jit(solution)/shard_map/ppermute | solution.py:17
  12.6 46.5 %collective-permute-start = (bf16[512,512]{1,0:T(8,128)(2,1)S(1)}, bf16[512,512]{1,0:T(8,128)(2,1)}, u32[]{:S(2)}, u32[]{:S(2)}) collective-permute-start(bf16[512,512]{1,0:T(8,128)(2,1)S(1)} %convolution_convert_fusion.2), channel_id=1, source_target_pairs={{0,2},{2,4},{4,6},{6,8},{8,10},{10,12},{12,14},{14,16},{16,18},{18... | collective-permute-start | bytes 1572872 | tf_op jit(solution)/shard_map/ppermute | solution.py:14
  21.0 37.2 %copy-start.6 = (s32[8192]{0:T(1024)S(1)}, s32[8192]{0:T(1024)}, u32[]{:S(2)}) copy-start(s32[8192]{0:T(1024)} %param.18) | copy-start | bytes 98308
  58.2 0.8 copy-start.4
  112.1 24.3 %copy-start.3 = (bf16[512,1024]{1,0:T(8,128)(2,1)S(1)}, bf16[512,1024]{1,0:T(8,128)(2,1)}, u32[]{:S(2)}) copy-start(bf16[512,1024]{1,0:T(8,128)(2,1)} %param.22) | copy-start | bytes 3145732
  112.3 18.2 %collective-permute-start.3 = (f32[512,512]{1,0:T(8,128)S(1)}, f32[512,512]{1,0:T(8,128)S(1)}, u32[]{:S(2)}, u32[]{:S(2)}) collective-permute-start(f32[512,512]{1,0:T(8,128)S(1)} %get-tuple-element.10), channel_id=1, source_target_pairs={{2,0},{4,2},{6,4},{8,6},{10,8},{12,10},{14,12},{16,14},{18,16},{20... | collective-permute-start | bytes 3145736 | tf_op jit(solution)/shard_map/ppermute | solution.py:25
  118.2 20.4 %copy-start.7 = (bf16[1024]{0:T(1024)(128)(2,1)S(1)}, bf16[1024]{0:T(1024)(128)(2,1)}, u32[]{:S(2)}) copy-start(bf16[1024]{0:T(1024)(128)(2,1)} %param.23) | copy-start | bytes 6148
  118.2 20.4 %copy-start.8 = (bf16[1024]{0:T(1024)(128)(2,1)S(1)}, bf16[1024]{0:T(1024)(128)(2,1)}, u32[]{:S(2)}) copy-start(bf16[1024]{0:T(1024)(128)(2,1)} %param.24) | copy-start | bytes 6148
  118.2 18.2 %collective-permute-start.2 = (f32[512,512]{1,0:T(8,128)S(1)}, f32[512,512]{1,0:T(8,128)S(1)}, u32[]{:S(2)}, u32[]{:S(2)}) collective-permute-start(f32[512,512]{1,0:T(8,128)S(1)} %get-tuple-element.9), channel_id=1, source_target_pairs={{0,2},{2,4},{4,6},{6,8},{8,10},{10,12},{12,14},{14,16},{16,18},{18... | collective-permute-start | bytes 3145736 | tf_op jit(solution)/shard_map/ppermute | solution.py:25
  138.5 172.1 %reduce-scatter.2.cloned.1.call-start = ((), (), s32[]{:S(2)}) async-start(), calls=%async_computation.2 | async-start | bytes 3145728 | tf_op jit(solution)/shard_map/reduce_scatter | solution.py:100
  215.1 1.2 copy-start.11
  215.5 1.6 copy-start.12
  216.4 1.5 copy-start.2
  218.9 16.6 %collective-permute-start.5 = (bf16[512,1024]{0,1:T(8,128)(2,1)}, bf16[512,1024]{0,1:T(8,128)(2,1)}, u32[]{:S(2)}, u32[]{:S(2)}) collective-permute-start(bf16[512,1024]{0,1:T(8,128)(2,1)} %pad_maximum_fusion.2), channel_id=1, source_target_pairs={{2,0},{4,2},{6,4},{8,6},{10,8},{12,10},{14,12},{16,14},{18,16},{20... | collective-permute-start | bytes 3145736 | tf_op jit(solution)/shard_map/ppermute | solution.py:17
  222.9 18.5 %collective-permute-start.4 = (bf16[512,1024]{0,1:T(8,128)(2,1)}, bf16[512,1024]{0,1:T(8,128)(2,1)}, u32[]{:S(2)}, u32[]{:S(2)}) collective-permute-start(bf16[512,1024]{0,1:T(8,128)(2,1)} %pad_maximum_fusion.2), channel_id=1, source_target_pairs={{0,2},{2,4},{4,6},{6,8},{8,10},{10,12},{12,14},{14,16},{16,18},{18... | collective-permute-start | bytes 3145736 | tf_op jit(solution)/shard_map/ppermute | solution.py:14
  249.7 1.9 copy-start.13
  271.7 3.6 %copy-start.10 = (bf16[1024]{0:T(1024)(128)(2,1)S(1)}, bf16[1024]{0:T(1024)(128)(2,1)}, u32[]{:S(2)}) copy-start(bf16[1024]{0:T(1024)(128)(2,1)} %param.29) | copy-start | bytes 6148
  271.7 41.2 %copy-start.1 = (bf16[1024,512]{1,0:T(8,128)(2,1)S(1)}, bf16[1024,512]{1,0:T(8,128)(2,1)}, u32[]{:S(2)}) copy-start(bf16[1024,512]{1,0:T(8,128)(2,1)} %param.19) | copy-start | bytes 3145732
Sparse Core Ops, SparseCore 0:
  138.7 74.2 all-reduce.1
  275.4 35.1 reduce-scatter.1
where the time goes:
time: 322 us; the launch traced here: 320 us
  waiting for transfers between devices  139 us (43%)
  local copies, waits for them, and re-layouts  74.3 us (23%)
  matrix products  57.1 us (18%)
  starting transfers between devices  19.5 us (6%)
  other arithmetic  15.9 us (5%)
  between operations  13.7 us (4%)
    psum x1, waiting for transfers between devices, body(): summed = lax.psum(message, 'feat')  74.3 us
    gather x1, local copies, waits for them, and re-layouts, body(): grid_proj[edge_src] + window[edge_dst].astype(jnp.float32)  37.2 us
    reduce_scatter x1, waiting for transfers between devices, body(): lax.psum_scatter(projected, 'feat', scatter_dimension=1, tiled=True)  35.2 us
    gather x1, local copies, waits for them, and re-layouts, body(): window[edge_dst].astype(jnp.float32)  33.8 us
    dot_general x1, matrix products, body(): partial_value = jnp.dot(onehot, hidden, preferred_element_type=jnp.float32)  18 us
    ppermute x2, waiting for transfers between devices, passed_along(): lax.ppermute(value, axis, [(source, source + steps) for source in range(i...  16.3 us
    dot_general x1, matrix products, body(): jnp.einsum('hqk,khd->qhd', attention, value_heads, preferred_element_type...  11.8 us
    concatenate x2, other arithmetic, with_halo(): block = jnp.concatenate([low, block, high], axis=dim)  9.57 us
  transfers between devices with their start and end apart: 8, of which 6 were waited for; matrix products, arithmetic and copies ran while one was open for 15% of the time, Pallas kernels for 0%

commit v1 on v0

--- a/solution.py
+++ b/solution.py
@@ -23,6 +23,10 @@
     count = lax.axis_size(axis)
     initial, last = (max(0, -steps), min(count, count - steps))
     return lax.ppermute(value, axis, [(source, source + steps) for source in range(initial, last)])
+
+
+def swapped(value):
+    return lax.ppermute(value, "feat", [(0, 1), (1, 0)])
 
 
 def own_columns(array, start, count):
@@ -51,6 +55,9 @@
     band_id = lax.axis_index("band")
     band_count = lax.axis_size("band")
     col_start = lax.axis_index("feat") * half_width
+    enc_other = swapped(w_enc_out)
+    out_other = swapped(own_columns(w_out, half_width - col_start, half_width))
+    out_own = own_columns(w_out, col_start, half_width)
     grid_proj = jnp.dot(grid_feat, w_grid, preferred_element_type=jnp.float32)
     mesh_proj = jnp.dot(mesh_feat, w_mesh, preferred_element_type=jnp.float32).astype(jnp.bfloat16)
     window = with_halo(mesh_proj, (("band", 0),), mesh_rows)
@@ -64,8 +71,11 @@
     from_above = passed_along(partial_value[2 * mesh_rows :], "band", 1)
     from_below = passed_along(partial_value[:mesh_rows], "band", -1)
     aggregate = partial_value[mesh_rows : 2 * mesh_rows] + from_above + from_below
-    message = jnp.dot(aggregate.astype(jnp.bfloat16), w_enc_out, preferred_element_type=jnp.float32)
-    summed = lax.psum(message, "feat")
+    own_half = aggregate.astype(jnp.bfloat16)
+    other_half = swapped(own_half)
+    summed = jnp.dot(own_half, w_enc_out, preferred_element_type=jnp.float32) + jnp.dot(
+        other_half, enc_other, preferred_element_type=jnp.float32
+    )
     latent = mesh_feat.astype(jnp.float32) + summed + b_enc.astype(jnp.float32)
     row_mean = jnp.mean(latent, axis=1, keepdims=True)
     row_var = jnp.mean((latent - row_mean) ** 2, axis=1, keepdims=True)
@@ -96,8 +106,9 @@
         "hqk,khd->qhd", attention, value_heads, preferred_element_type=jnp.float32
     )
     mixed_heads = mixed_heads.reshape(mesh_rows, half_width).astype(jnp.bfloat16)
-    projected = jnp.dot(mixed_heads, w_out, preferred_element_type=jnp.float32)
-    out_part = lax.psum_scatter(projected, "feat", scatter_dimension=1, tiled=True)
+    out_part = jnp.dot(mixed_heads, out_own, preferred_element_type=jnp.float32) + jnp.dot(
+        swapped(mixed_heads), out_other, preferred_element_type=jnp.float32
+    )
     result = latent_half + out_part + own_columns(b_out, col_start, half_width).astype(jnp.float32)
     return result.astype(jnp.bfloat16)
 

time: 322 us -> 234 us (0.73)
  waiting for transfers between devices: 139 us -> 46.8 us
  starting transfers between devices: 19.5 us -> 40.9 us
  between operations: 13.7 us -> 0.33 us
  other arithmetic: 15.9 us -> 11.8 us
    psum x1 -> x0, waiting for transfers between devices: 74.3 us -> none  [body(): summed = lax.psum(message, 'feat')]
    reduce_scatter x1 -> x0, waiting for transfers between devices: 35.2 us -> none  [body(): lax.psum_scatter(projected, 'feat', scatter_dimension=1, tiled=True)]
    ppermute x0 -> x4, waiting for transfers between devices: none -> 23.5 us  [swapped(): return lax.ppermute(value, 'feat', [(0, 1), (1, 0)])]
    ppermute x2, starting transfers between devices: 7.59 us -> 19.8 us  [with_halo(): lax.ppermute(lax.slice_in_dim(block, 0, width, axis=dim), axis, backward)]
    ppermute x0 -> x4, starting transfers between devices: none -> 9.33 us  [swapped(): return lax.ppermute(value, 'feat', [(0, 1), (1, 0)])]
    ppermute x2, waiting for transfers between devices: 7.39 us -> 3.41 us  [with_halo(): lax.ppermute(lax.slice_in_dim(block, 0, width, axis=dim), axis, backward)]
  transfers between devices with their start and end apart: 8 -> 10, of which waited for: 6 -> 7; matrix products, arithmetic and copies ran while one was open for 15% -> 35% of each run, Pallas kernels for 0% -> 0%
where the time goes in v1:
time: 234 us; the launch traced here: 233 us
  local copies, waits for them, and re-layouts  76 us (32%)
  matrix products  57.6 us (25%)
  waiting for transfers between devices  46.8 us (20%)
  starting transfers between devices  40.9 us (17%)
  other arithmetic  11.8 us (5%)
    gather x1, local copies, waits for them, and re-layouts, body(): grid_proj[edge_src] + window[edge_dst].astype(jnp.float32)  37.1 us
    gather x1, local copies, waits for them, and re-layouts, body(): window[edge_dst].astype(jnp.float32)  33.6 us
    ppermute x4, waiting for transfers between devices, swapped(): return lax.ppermute(value, 'feat', [(0, 1), (1, 0)])  23.5 us
    ppermute x2, starting transfers between devices, with_halo(): lax.ppermute(lax.slice_in_dim(block, 0, width, axis=dim), axis, backward)  19.8 us
    dot_general x1, matrix products, body(): partial_value = jnp.dot(onehot, hidden, preferred_element_type=jnp.float32)  18 us
    ppermute x2, waiting for transfers between devices, passed_along(): lax.ppermute(value, axis, [(source, source + steps) for source in range(i...  13.9 us
    dot_general x1, matrix products, body(): jnp.einsum('hqk,khd->qhd', attention, value_heads, preferred_element_type...  12.1 us
    concatenate x2, other arithmetic, with_halo(): block = jnp.concatenate([low, block, high], axis=dim)  9.57 us
  transfers between devices with their start and end apart: 10, of which 7 were waited for; matrix products, arithmetic and copies ran while one was open for 35% of the time, Pallas kernels for 0%

profile of v1, /device:TPU:40, one launch (start us, length us, event | category | flops | bytes accessed | tf_op | source)
XLA Modules:
  0.0 233.4 jit_solution(4944780450429105732)
XLA Ops:
  0.0 2.3 convolution_convert_fusion.2
  2.4 3.7 %collective-permute-start.1 = (bf16[512,512]{1,0:T(8,128)(2,1)S(1)}, bf16[512,512]{1,0:T(8,128)(2,1)S(1)}, u32[]{:S(2)}, u32[]{:S(2)}) collective-permute-start(bf16[512,512]{1,0:T(8,128)(2,1)S(1)} %convolution_convert_fusion.2), channel_id=1, source_target_pairs={{2,0},{4,2},{6,4},{8,6},{10,8},{12,10},{14,12},{16,14},{18,16},{20... | collective-permute-start | bytes 1572872 | tf_op jit(solution)/shard_map/ppermute | solution.py:17
  6.0 1.9 collective-permute-start
  8.0 6.5 %fusion.39 = f32[2048,512]{1,0:T(8,128)} fusion(bf16[2048,1024]{1,0:T(8,128)(2,1)} %param.15, bf16[1024,512]{1,0:T(8,128)(2,1)S(1)} %copy-done), kind=kOutput, calls=%fused_computation.63 | convolution fusion | flops 2147483648 | bytes 9437184 | tf_op jit(solution)/shard_map/dot_general | solution.py:61
  14.5 0.0 copy-start.7
  14.5 37.1 %gather_fusion = f32[8192,512]{1,0:T(8,128)} fusion(f32[2048,512]{1,0:T(8,128)} %fusion.39, s32[8192]{0:T(1024)S(1)} %fusion.19), kind=kCustom, calls=%fused_computation | custom fusion | bytes 33587200 | tf_op jit(solution)/shard_map/gather | solution.py:65
  51.6 0.0 copy-start.5
  51.7 0.8 copy-done.5
  52.4 1.3 pad_maximum_fusion.1
  53.8 33.6 %gather_fusion.1 = bf16[8192,512]{1,0:T(8,128)(2,1)} fusion(bf16[1536,512]{1,0:T(8,128)(2,1)S(1)} %pad_maximum_fusion.1, s32[8192]{0:T(1024)S(1)} %fusion.20), kind=kCustom, calls=%fused_computation.1 | custom fusion | bytes 16809984 | tf_op jit(solution)/shard_map/gather | solution.py:65
  87.3 18.0 %fusion.1 = f32[1536,512]{1,0:T(8,128)S(1)} fusion(s32[8192]{0:T(1024)S(1)} %copy-done.7, f32[8192,512]{1,0:T(8,128)} %gather_fusion, bf16[8192,512]{1,0:T(8,128)(2,1)} %gather_fusion.1, f32[512]{0:T(512)S(1)} %convert_element_type.58), kind=kOutput, calls=%fused_computation.4 | convolution fusion | flops 12931039232 | bytes 28346368 | tf_op jit(solution)/shard_map/dot_general | solution.py:70
  105.4 0.0 copy-start.9
  105.4 0.2 fusion.36
  105.6 5.9 %collective-permute-start.3 = (f32[512,512]{1,0:T(8,128)S(1)}, f32[512,512]{1,0:T(8,128)S(1)}, u32[]{:S(2)}, u32[]{:S(2)}) collective-permute-start(f32[512,512]{1,0:T(8,128)S(1)} %get-tuple-element.8), channel_id=1, source_target_pairs={{2,0},{4,2},{6,4},{8,6},{10,8},{12,10},{14,12},{16,14},{18,16},{20... | collective-permute-start | bytes 3145736 | tf_op jit(solution)/shard_map/ppermute | solution.py:25
  111.4 0.0 copy-start.3
  111.5 2.1 collective-permute-start.2
  113.5 2.4 %collective-permute-start.5 = (bf16[512,1024]{1,0:T(8,128)(2,1)S(1)}, bf16[512,1024]{1,0:T(8,128)(2,1)S(1)}, u32[]{:S(2)}, u32[]{:S(2)}) collective-permute-start(bf16[512,1024]{1,0:T(8,128)(2,1)S(1)} %copy-done.4), channel_id=1, source_target_pairs={{0,1},{1,0},{2,3},{3,2},{4,5},{5,4},{6,7},{7,6},{8,9},{9,8},{10,11... | collective-permute-start | bytes 3145736 | tf_op jit(solution)/shard_map/ppermute | solution.py:29
  115.9 7.8 %collective-permute-done.3 = f32[512,512]{1,0:T(8,128)S(1)} collective-permute-done((f32[512,512]{1,0:T(8,128)S(1)}, f32[512,512]{1,0:T(8,128)S(1)}, u32[]{:S(2)}, u32[]{:S(2)}) %collective-permute-start.3) | collective-permute-done | bytes 1048608 | tf_op jit(solution)/shard_map/ppermute | solution.py:25
  123.7 6.1 %collective-permute-done.2 = f32[512,512]{1,0:T(8,128)S(1)} collective-permute-done((f32[512,512]{1,0:T(8,128)S(1)}, f32[512,512]{1,0:T(8,128)S(1)}, u32[]{:S(2)}, u32[]{:S(2)}) %collective-permute-start.2) | collective-permute-done | bytes 1048608 | tf_op jit(solution)/shard_map/ppermute | solution.py:25
  129.8 0.4 fusion.12
  130.2 2.4 %collective-permute-start.4 = (bf16[512,512]{1,0:T(8,128)(2,1)S(1)}, bf16[512,512]{1,0:T(8,128)(2,1)S(1)}, u32[]{:S(2)}, u32[]{:S(2)}) collective-permute-start(bf16[512,512]{1,0:T(8,128)(2,1)S(1)} %fusion.12), channel_id=1, source_target_pairs={{0,1},{1,0},{2,3},{3,2},{4,5},{5,4},{6,7},{7,6},{8,9},{9,8},{10,11... | collective-permute-start | bytes 1572872 | tf_op jit(solution)/shard_map/ppermute | solution.py:29
  132.6 8.6 %collective-permute-done.5 = bf16[512,1024]{1,0:T(8,128)(2,1)S(1)} collective-permute-done((bf16[512,1024]{1,0:T(8,128)(2,1)S(1)}, bf16[512,1024]{1,0:T(8,128)(2,1)S(1)}, u32[]{:S(2)}, u32[]{:S(2)}) %collective-permute-start.5) | collective-permute-done | bytes 1048608 | tf_op jit(solution)/shard_map/ppermute | solution.py:29
  141.2 8.0 %collective-permute-done.4 = bf16[512,512]{1,0:T(8,128)(2,1)S(1)} collective-permute-done((bf16[512,512]{1,0:T(8,128)(2,1)S(1)}, bf16[512,512]{1,0:T(8,128)(2,1)S(1)}, u32[]{:S(2)}, u32[]{:S(2)}) %collective-permute-start.4) | collective-permute-done | bytes 524320 | tf_op jit(solution)/shard_map/ppermute | solution.py:29
  149.2 0.7 fusion.40
  149.9 0.9 fusion.37
  150.8 0.3 multiply_reduce_fusion
  151.2 0.3 multiply_convert_fusion.2
  151.5 0.5 copy-done.12
  152.1 0.8 convolution_convert_fusion
  152.8 0.8 convolution_convert_fusion.1
  153.6 1.0 pad_maximum_fusion.2
  154.6 16.2 %collective-permute-start.7 = (bf16[512,1024]{0,1:T(8,128)(2,1)}, bf16[512,1024]{0,1:T(8,128)(2,1)}, u32[]{:S(2)}, u32[]{:S(2)}) collective-permute-start(bf16[512,1024]{0,1:T(8,128)(2,1)} %pad_maximum_fusion.2), channel_id=1, source_target_pairs={{2,0},{4,2},{6,4},{8,6},{10,8},{12,10},{14,12},{16,14},{18,16},{20... | collective-permute-start | bytes 3145736 | tf_op jit(solution)/shard_map/ppermute | solution.py:17
  170.8 1.9 collective-permute-start.6
  172.8 1.9 constant_dynamic-slice_fusion
  174.6 2.3 collective-permute-start.9
  176.9 3.1 %fusion.10 = bf16[512,512]{0,1:T(8,128)(2,1)} fusion(bf16[512,1024]{1,0:T(8,128)(2,1)} %copy-done.2, bf16[1024,512]{1,0:T(8,128)(2,1)} %param.25), kind=kOutput, calls=%fused_computation.23 | convolution fusion | flops 537395200 | bytes 2621440 | tf_op jit(solution)/shard_map/dot_general | solution.py:86
  180.0 3.4 %collective-permute-done.7 = bf16[512,1024]{0,1:T(8,128)(2,1)} collective-permute-done((bf16[512,1024]{0,1:T(8,128)(2,1)}, bf16[512,1024]{0,1:T(8,128)(2,1)}, u32[]{:S(2)}, u32[]{:S(2)}) %collective-permute-start.7) | collective-permute-done | bytes 1048608 | tf_op jit(solution)/shard_map/ppermute | solution.py:17
  183.4 5.9 %collective-permute-done.6 = bf16[512,1024]{0,1:T(8,128)(2,1)} collective-permute-done((bf16[512,1024]{0,1:T(8,128)(2,1)}, bf16[512,1024]{0,1:T(8,128)(2,1)}, u32[]{:S(2)}, u32[]{:S(2)}) %collective-permute-start.6) | collective-permute-done | bytes 1048608 | tf_op jit(solution)/shard_map/ppermute | solution.py:14
  189.4 8.3 %pad_maximum_fusion = bf16[1536,1024]{0,1:T(8,128)(2,1)S(1)} fusion(bf16[512,1024]{0,1:T(8,128)(2,1)} %collective-permute-done.7, bf16[512,512]{0,1:T(8,128)(2,1)S(1)} %convolution_convert_fusion, bf16[512,512]{0,1:T(8,128)(2,1)S(1)} %convolution_convert_fusion.1, bf16[512,1024]{0,1:T(8,128)(2,1)} %collective-permute-done.6), kind=kLoop, calls=%fused_computation.14 | loop fusion | flops 12582912 | bytes 6291456 | tf_op jit(solution)/shard_map/concatenate | solution.py:18
  197.7 1.8 fusion.35
  199.5 8.3 %fusion.38 = f32[8,512]{1,0:T(8,128)S(1)} fusion(pred[1536]{0:T(1024)(128)(4,1)S(1)} %fusion.27, bf16[512,8,64]{0,2,1:T(8,128)(2,1)S(1)} %bitcast.34, bf16[1536,8,64]{0,2,1:T(8,128)(2,1)} %bitcast.28), kind=kOutput, calls=%fused_computation.62 | convolution fusion | flops 824182272 | bytes 2115072 | tf_op jit(solution)/shard_map/sub | solution.py:102
  207.8 0.0 copy-start.1
  207.8 12.1 %fusion.9 = bf16[8,64,512]{2,1,0:T(8,128)(2,1)} fusion(bf16[1536,8,64]{0,2,1:T(8,128)(2,1)} %bitcast.30, f32[8,512]{1,0:T(8,128)S(1)} %fusion.38, pred[1536]{0:T(1024)(128)(4,1)S(1)} %fusion.27, bf16[512,8,64]{0,2,1:T(8,128)(2,1)} %bitcast.33, bf16[1536,8,64]{0,2,1:T(8,128)(2,1)} %bitcast.29), kind=kOutput, calls=%fused_computation.22 | convolution fusion | flops 1636046336 | bytes 4212224 | tf_op jit(solution)/shard_map/hqk,khd->qhd/dot_general | solution.py:105
  219.9 2.3 collective-permute-start.8
  222.2 0.1 dynamic-slice_convert_fusion
  222.3 1.7 fusion.17
  224.0 7.0 %collective-permute-done.8 = bf16[512,512]{0,1:T(8,128)(2,1)} collective-permute-done((bf16[512,512]{0,1:T(8,128)(2,1)}, bf16[512,512]{0,1:T(8,128)(2,1)}, u32[]{:S(2)}, u32[]{:S(2)}) %collective-permute-start.8) | collective-permute-done | bytes 524320 | tf_op jit(solution)/shard_map/ppermute | solution.py:29
  230.9 2.5 %add_convert_fusion = bf16[512,512]{1,0:T(8,128)(2,1)} fusion(f32[512,1024]{1,0:T(8,128)S(1)} %get-tuple-element.10, s32[]{:T(128)S(6)} %select_n.29, f32[512]{0:T(512)S(1)} %dynamic-slice_convert_fusion, f32[512,512]{1,0:T(8,128)S(1)} %fusion.17, bf16[512,512]{0,1:T(8,128)(2,1)} %collective-permute-done.8, bf16[512,512]{1,0:T(8,128)(2,1)} %collective-permute-done.9), kind=kOutput, calls=%fused_computation.31 | convolution fusion | flops 269484032 | bytes 3672068 | tf_op jit(solution)/shard_map/dot_general | solution.py:109
  (34 shorter events, 0.1 us)
Async XLA Ops:
  0.0 8.0 %copy-start = (bf16[1024,512]{1,0:T(8,128)(2,1)S(1)}, bf16[1024,512]{1,0:T(8,128)(2,1)}, u32[]{:S(2)}) copy-start(bf16[1024,512]{1,0:T(8,128)(2,1)} %param.19) | copy-start | bytes 3145732
  2.3 12.1 %copy-start.10 = (bf16[512]{0:T(512)(128)(2,1)S(1)}, bf16[512]{0:T(512)(128)(2,1)}, u32[]{:S(2)}) copy-start(bf16[512]{0:T(512)(128)(2,1)} %param.21) | copy-start | bytes 3076
  2.4 12.1 %copy-start.6 = (s32[8192]{0:T(1024)S(1)}, s32[8192]{0:T(1024)}, u32[]{:S(2)}) copy-start(s32[8192]{0:T(1024)} %param.17) | copy-start | bytes 98308
  2.4 49.3 %collective-permute-start.1 = (bf16[512,512]{1,0:T(8,128)(2,1)S(1)}, bf16[512,512]{1,0:T(8,128)(2,1)S(1)}, u32[]{:S(2)}, u32[]{:S(2)}) collective-permute-start(bf16[512,512]{1,0:T(8,128)(2,1)S(1)} %convolution_convert_fusion.2), channel_id=1, source_target_pairs={{2,0},{4,2},{6,4},{8,6},{10,8},{12,10},{14,12},{16,14},{18,16},{20... | collective-permute-start | bytes 1572872 | tf_op jit(solution)/shard_map/ppermute | solution.py:17
  6.0 46.4 %collective-permute-start = (bf16[512,512]{1,0:T(8,128)(2,1)S(1)}, bf16[512,512]{1,0:T(8,128)(2,1)}, u32[]{:S(2)}, u32[]{:S(2)}) collective-permute-start(bf16[512,512]{1,0:T(8,128)(2,1)S(1)} %convolution_convert_fusion.2), channel_id=1, source_target_pairs={{0,2},{2,4},{4,6},{6,8},{8,10},{10,12},{12,14},{14,16},{16,18},{18... | collective-permute-start | bytes 1572872 | tf_op jit(solution)/shard_map/ppermute | solution.py:14
  14.5 37.2 %copy-start.7 = (s32[8192]{0:T(1024)S(1)}, s32[8192]{0:T(1024)}, u32[]{:S(2)}) copy-start(s32[8192]{0:T(1024)} %param.18) | copy-start | bytes 98308
  51.6 0.8 copy-start.5
  105.3 8.2 %copy-start.4 = (bf16[512,1024]{1,0:T(8,128)(2,1)S(1)}, bf16[512,1024]{1,0:T(8,128)(2,1)}, u32[]{:S(2)}) copy-start(bf16[512,1024]{1,0:T(8,128)(2,1)} %param.22) | copy-start | bytes 3145732
  105.4 27.2 %copy-start.8 = (bf16[1024]{0:T(1024)(128)(2,1)S(1)}, bf16[1024]{0:T(1024)(128)(2,1)}, u32[]{:S(2)}) copy-start(bf16[1024]{0:T(1024)(128)(2,1)} %param.23) | copy-start | bytes 6148
  105.4 27.2 %copy-start.9 = (bf16[1024]{0:T(1024)(128)(2,1)S(1)}, bf16[1024]{0:T(1024)(128)(2,1)}, u32[]{:S(2)}) copy-start(bf16[1024]{0:T(1024)(128)(2,1)} %param.24) | copy-start | bytes 6148
  105.6 18.2 %collective-permute-start.3 = (f32[512,512]{1,0:T(8,128)S(1)}, f32[512,512]{1,0:T(8,128)S(1)}, u32[]{:S(2)}, u32[]{:S(2)}) collective-permute-start(f32[512,512]{1,0:T(8,128)S(1)} %get-tuple-element.8), channel_id=1, source_target_pairs={{2,0},{4,2},{6,4},{8,6},{10,8},{12,10},{14,12},{16,14},{18,16},{20... | collective-permute-start | bytes 3145736 | tf_op jit(solution)/shard_map/ppermute | solution.py:25
  111.4 38.5 %copy-start.3 = (bf16[512,1024]{1,0:T(8,128)(2,1)S(1)}, bf16[512,1024]{1,0:T(8,128)(2,1)}, u32[]{:S(2)}) copy-start(bf16[512,1024]{1,0:T(8,128)(2,1)} %param.16) | copy-start | bytes 3145732
  111.5 18.4 %collective-permute-start.2 = (f32[512,512]{1,0:T(8,128)S(1)}, f32[512,512]{1,0:T(8,128)S(1)}, u32[]{:S(2)}, u32[]{:S(2)}) collective-permute-start(f32[512,512]{1,0:T(8,128)S(1)} %get-tuple-element.7), channel_id=1, source_target_pairs={{0,2},{2,4},{4,6},{6,8},{8,10},{10,12},{12,14},{14,16},{16,18},{18... | collective-permute-start | bytes 3145736 | tf_op jit(solution)/shard_map/ppermute | solution.py:25
  113.5 27.7 %collective-permute-start.5 = (bf16[512,1024]{1,0:T(8,128)(2,1)S(1)}, bf16[512,1024]{1,0:T(8,128)(2,1)S(1)}, u32[]{:S(2)}, u32[]{:S(2)}) collective-permute-start(bf16[512,1024]{1,0:T(8,128)(2,1)S(1)} %copy-done.4), channel_id=1, source_target_pairs={{0,1},{1,0},{2,3},{3,2},{4,5},{5,4},{6,7},{7,6},{8,9},{9,8},{10,11... | collective-permute-start | bytes 3145736 | tf_op jit(solution)/shard_map/ppermute | solution.py:29
  130.2 19.0 %collective-permute-start.4 = (bf16[512,512]{1,0:T(8,128)(2,1)S(1)}, bf16[512,512]{1,0:T(8,128)(2,1)S(1)}, u32[]{:S(2)}, u32[]{:S(2)}) collective-permute-start(bf16[512,512]{1,0:T(8,128)(2,1)S(1)} %fusion.12), channel_id=1, source_target_pairs={{0,1},{1,0},{2,3},{3,2},{4,5},{5,4},{6,7},{7,6},{8,9},{9,8},{10,11... | collective-permute-start | bytes 1572872 | tf_op jit(solution)/shard_map/ppermute | solution.py:29
  150.8 1.2 copy-start.12
  151.2 1.6 copy-start.13
  152.1 1.5 copy-start.2
  154.6 28.8 %collective-permute-start.7 = (bf16[512,1024]{0,1:T(8,128)(2,1)}, bf16[512,1024]{0,1:T(8,128)(2,1)}, u32[]{:S(2)}, u32[]{:S(2)}) collective-permute-start(bf16[512,1024]{0,1:T(8,128)(2,1)} %pad_maximum_fusion.2), channel_id=1, source_target_pairs={{2,0},{4,2},{6,4},{8,6},{10,8},{12,10},{14,12},{16,14},{18,16},{20... | collective-permute-start | bytes 3145736 | tf_op jit(solution)/shard_map/ppermute | solution.py:17
  170.8 18.5 %collective-permute-start.6 = (bf16[512,1024]{0,1:T(8,128)(2,1)}, bf16[512,1024]{0,1:T(8,128)(2,1)}, u32[]{:S(2)}, u32[]{:S(2)}) collective-permute-start(bf16[512,1024]{0,1:T(8,128)(2,1)} %pad_maximum_fusion.2), channel_id=1, source_target_pairs={{0,2},{2,4},{4,6},{6,8},{8,10},{10,12},{12,14},{14,16},{16,18},{18... | collective-permute-start | bytes 3145736 | tf_op jit(solution)/shard_map/ppermute | solution.py:14
  174.6 49.3 %collective-permute-start.9 = (bf16[512,512]{1,0:T(8,128)(2,1)}, bf16[512,512]{1,0:T(8,128)(2,1)}, u32[]{:S(2)}, u32[]{:S(2)}) collective-permute-start(bf16[512,512]{1,0:T(8,128)(2,1)} %constant_dynamic-slice_fusion), channel_id=1, source_target_pairs={{0,1},{1,0},{2,3},{3,2},{4,5},{5,4},{6,7},{7,6},{8,9},{9,8},{10,11... | collective-permute-start | bytes 1572872 | tf_op jit(solution)/shard_map/ppermute | solution.py:29
  197.6 1.9 copy-start.14
  207.8 14.4 %copy-start.11 = (bf16[1024]{0:T(1024)(128)(2,1)S(1)}, bf16[1024]{0:T(1024)(128)(2,1)}, u32[]{:S(2)}) copy-start(bf16[1024]{0:T(1024)(128)(2,1)} %param.29) | copy-start | bytes 6148
  207.8 25.6 %copy-start.1 = (bf16[1024,512]{1,0:T(8,128)(2,1)S(1)}, bf16[1024,512]{1,0:T(8,128)(2,1)}, u32[]{:S(2)}) copy-start(bf16[1024,512]{1,0:T(8,128)(2,1)} %param.19) | copy-start | bytes 3145732
  219.9 11.0 %collective-permute-start.8 = (bf16[512,512]{0,1:T(8,128)(2,1)}, bf16[512,512]{0,1:T(8,128)(2,1)}, u32[]{:S(2)}, u32[]{:S(2)}) collective-permute-start(bf16[512,512]{0,1:T(8,128)(2,1)} %bitcast.31), channel_id=1, source_target_pairs={{0,1},{1,0},{2,3},{3,2},{4,5},{5,4},{6,7},{7,6},{8,9},{9,8},{10,11... | collective-permute-start | bytes 1572872 | tf_op jit(solution)/shard_map/ppermute | solution.py:29
